TPU v7x, 512 devices: a whole 4x8x8 slice. The times are simulated.
512 devices in a mesh: feed: 32 (over z_hi, y), tm: 16 (over x, z_lo, core).
Axes of the slice: x: 4, y: 8, z: 8 (z_hi: 4, z_lo: 2; z = z_hi * 2 + z_lo), core: 2. Of those that a mesh axis runs over, the one named last changes fastest.
Arguments:
- voltages: bfloat16 [2048, 262144], P('feed', 'tm'), may hold values from -6 to 6
- pfb_coeffs: float32 [4, 2048], replicated, may hold values from 0.25 to 1.75
- flags: int32 [128, 64], P('tm'), may hold values from 0 to 1, as said below
- channel_order: int32 [64], replicated, may hold values from 0 to 63, each once
Outputs:
- vis_real: bfloat16 [64, 2048, 2048], P('feed', 'tm')
- vis_imag: bfloat16 [64, 2048, 2048], P('feed', 'tm')
Inputs may be any that keep to these rules, and one draw needn't show every extreme that they name: `flags`: some window channels are flagged in every spectrum.
All inputs are finite; a program needn't handle non-finite values.
Results may differ from a plain program's by a relative error of at most 0.0059.
Values may be sent and summed in bfloat16 or wider, within the bound.
A program may use at most 64 MiB of HBM per device.

v0:
```python
import jax
import jax.numpy as jnp
from jax import lax
from jax.sharding import PartitionSpec as P

CHAN0 = 448


def shifted(block, axis, distance):
    devices = range(lax.axis_size(axis))
    route = [(i - distance, i) for i in devices if i - distance in devices]
    return lax.ppermute(block, axis, route)


def make_table(coeffs, order, chan_first):
    tap_count, frame_len = coeffs.shape
    window = order.shape[0]
    sample = jnp.arange(frame_len, dtype=jnp.int32)
    freq = chan_first + order
    phase = freq[None, :] * sample[:, None] % frame_len
    angle = phase.astype(jnp.float32) * (2.0 * jnp.pi / frame_len)
    trig = jnp.stack([jnp.cos(angle), -jnp.sin(angle)], axis=2).reshape(frame_len, 2 * window)
    scale = (tap_count * frame_len / 2.0) ** (-0.5)
    table = coeffs[:, :, None] * trig[None, :, :] * scale
    return table.reshape(tap_count * frame_len, 2 * window).astype(jnp.bfloat16)


def correlate(part, row_start, row_count):
    chan_pairs, spec_count, input_count = part.shape
    pairs = part.reshape(chan_pairs // 2, 2, spec_count, input_count)
    real_part = pairs[:, 0]
    imag_part = pairs[:, 1]
    full = jnp.concatenate([real_part, imag_part], axis=1)
    swapped = jnp.concatenate([imag_part, -real_part], axis=1)
    left = jnp.concatenate(
        [
            lax.dynamic_slice_in_dim(full, row_start, row_count, 2),
            lax.dynamic_slice_in_dim(swapped, row_start, row_count, 2),
        ],
        axis=2,
    )
    return jnp.einsum("ckr,ckj->crj", left, full, preferred_element_type=jnp.float32)


def body(voltages, pfb_coeffs, flags, channel_order):
    input_local, sample_count = voltages.shape
    tap_count, frame_len = pfb_coeffs.shape
    spec_local = sample_count // frame_len
    window = channel_order.shape[0]
    tail = voltages[:, sample_count - (tap_count - 1) * frame_len :]
    earlier = shifted(tail, "tm", 1)
    extended = jnp.concatenate([earlier, voltages], axis=1).reshape(
        input_local, spec_local + tap_count - 1, frame_len
    )
    frames = jnp.concatenate([extended[:, t : t + spec_local, :] for t in range(tap_count)], axis=2)
    table = make_table(pfb_coeffs, channel_order, CHAN0)
    raw = jnp.einsum("isk,kc->csi", frames, table, preferred_element_type=jnp.float32)
    good = jnp.take(flags, channel_order, axis=1).astype(jnp.float32)
    mask = jnp.repeat(good.T, 2, axis=0)
    spectra = (raw * mask[:, :, None]).astype(jnp.bfloat16)
    counts_all = lax.psum(jnp.sum(good, axis=0), "tm")
    chan_own = window // lax.axis_size("feed")
    own_counts = lax.dynamic_slice_in_dim(counts_all, lax.axis_index("feed") * chan_own, chan_own)
    denom = jnp.maximum(own_counts, 1.0)
    row_count = input_local * lax.axis_size("feed") // lax.axis_size("tm")
    row_start = lax.axis_index("tm") * row_count
    turned = lax.all_to_all(spectra, "feed", split_axis=0, concat_axis=2, tiled=True)
    every_spec = lax.all_gather(turned, "tm", axis=1, tiled=True)
    total = correlate(every_spec, row_start, row_count)
    scaled = total / denom[:, None, None]
    vis_real = scaled[:, :row_count].astype(jnp.bfloat16)
    vis_imag = scaled[:, row_count:].astype(jnp.bfloat16)
    return (vis_real, vis_imag)


def solution(mesh):
    return jax.shard_map(
        body,
        mesh=mesh,
        in_specs=(P("feed", "tm"), P(), P("tm", None), P()),
        out_specs=(P("feed", "tm", None), P("feed", "tm", None)),
        check_vma=False,
    )
```

profile of v0, /device:TPU:1, one launch (start us, length us, event | category | flops | bytes accessed | tf_op | source)
XLA Modules:
  0.0 118.2 jit_solution(4359193663645784458)
XLA Ops:
  7.2 0.0 all-gather.2.cloned.1.call-start
  7.2 1.2 %slice.29 = bf16[64,6144]{1,0:T(8,128)(2,1)S(1)} slice(bf16[64,16384]{1,0:T(8,128)(2,1)} %param.4), slice={[0:64], [10240:16384]} | slice | bytes 1572864 | tf_op jit(solution)/shard_map/slice | solution.py:50
  8.4 5.4 %collective-permute-start = (bf16[64,6144]{1,0:T(8,128)(2,1)S(1)}, bf16[64,6144]{1,0:T(8,128)(2,1)}, u32[]{:S(2)}, u32[]{:S(2)}) collective-permute-start(bf16[64,6144]{1,0:T(8,128)(2,1)S(1)} %slice.29), channel_id=1, source_target_pairs={{0,1},{1,2},{2,3},{3,4},{4,5},{5,6},{6,7},{7,8},{8,9},{9,10},{10,1... | collective-permute-start | bytes 2359304 | tf_op jit(solution)/shard_map/ppermute | solution.py:12
  13.8 0.7 compare_select_fusion
  14.5 2.1 %fusion.35 = (f32[2048,64,1]{0,1,2:T(8,128)S(1)}, f32[2048,64,1]{0,1,2:T(8,128)S(1)}) fusion(s32[64]{0:T(128)S(1)} %get-tuple-element.15), kind=kLoop, calls=%fused_computation.39 | loop fusion | flops 1966080 | bytes 1048832 | tf_op jit(solution)/shard_map/cos | solution.py:22
  16.6 0.1 pad_maximum_fusion.3
  16.7 0.8 copy.33
  17.5 0.0 copy-start.3
  17.5 0.0 copy-start.4
  17.5 0.0 copy-start.5
  17.5 0.7 mul.92
  18.3 0.3 copy.34
  18.6 0.0 copy-done.3
  18.6 0.0 copy-done.4
  18.6 0.1 copy.39
  18.7 0.6 gather_fusion
  19.3 0.0 copy-done.5
  19.3 0.2 fusion.41
  19.6 0.0 copy-start.1
  19.6 2.4 %fusion.9 = bf16[8192,128]{1,0:T(8,128)(2,1)} fusion(f32[2048,128]{1,0:T(8,128)S(1)} %copy.34, f32[8192]{0:T(1024)S(1)} %bitcast.42), kind=kLoop, calls=%fused_computation.11 | loop fusion | flops 3145728 | bytes 3178496 | tf_op jit(solution)/shard_map/convert_element_type | solution.py:25
  22.0 0.7 collective-permute-done
  22.7 0.0 copy-done.1
  22.7 1.3 %pad_maximum_fusion = bf16[64,22528]{1,0:T(8,128)(2,1)S(1)} fusion(bf16[64,16384]{1,0:T(8,128)(2,1)S(1)} %copy-done.1, bf16[64,6144]{1,0:T(8,128)(2,1)} %collective-permute-done), kind=kLoop, calls=%fused_computation.13 | loop fusion | flops 5767168 | bytes 5767168 | tf_op jit(solution)/shard_map/concatenate | solution.py:52
  24.0 3.5 %reshape.119 = bf16[64,11,2048]{2,1,0:T(8,128)(2,1)} reshape(bf16[64,22528]{1,0:T(8,128)(2,1)S(1)} %pad_maximum_fusion) | data formatting | bytes 5767168 | tf_op jit(solution)/shard_map/reshape | solution.py:52
  27.5 8.6 %fusion.42 = (bf16[64,8,2048]{2,1,0:T(8,128)(2,1)S(1)}, bf16[64,8,2048]{2,1,0:T(8,128)(2,1)S(1)}, bf16[64,8,2048]{2,1,0:T(8,128)(2,1)S(1)}, bf16[64,8,2048]{2,1,0:T(8,128)(2,1)S(1)}) fusion(bf16[64,11,2048]{2,1,0:T(8,128)(2,1)} %reshape.119), kind=kLoop, calls=%fused_computation.52 | loop fusion | bytes 16777216 | tf_op jit(solution)/shard_map/slice | solution.py:55
  36.1 1.2 copy.50
  37.3 1.2 copy.49
  38.4 1.2 copy.48
  39.6 0.0 copy-start.2
  39.6 1.2 copy.47
  40.8 0.4 copy-done.2
  41.2 2.8 %fusion.21 = bf16[128,8,64]{0,2,1:T(8,128)(2,1)S(1)} fusion(bf16[64,8,2048]{2,0,1:T(8,128)(2,1)S(1)} %copy.50, bf16[64,8,2048]{2,0,1:T(8,128)(2,1)S(1)} %copy.49, bf16[64,8,2048]{2,0,1:T(8,128)(2,1)S(1)} %copy.48, bf16[64,8,2048]{2,0,1:T(8,128)(2,1)S(1)} %copy.47, bf16[8192,128]{1,0:T(8,128)(2,1)S(1)} %copy-done.2, f32[128,8]{0,1:T(8,128)S(1)} %copy.40), kind=kOutput, calls=%fused_computation.22 | convolution fusion | flops 1107427328 | bytes 10620928 | tf_op jit(solution)/shard_map/isk,kc->csi/dot_general | solution.py:57
  44.0 0.2 copy.41
  44.2 0.2 reshape.131
  44.4 26.8 %all_to_all.18 = bf16[32,2,1024]{2,1,0:T(2,128)(2,1)S(1)} all-to-all(bf16[32,2,1024]{2,1,0:T(2,128)(2,1)S(1)} %reshape.131), channel_id=1, replica_groups=mesh['feed'=32,'tm'=16] {'feed'}, dimensions={0} | all-to-all | bytes 262144 | tf_op jit(solution)/shard_map/all_to_all | solution.py:67
  71.2 0.2 reshape.132
  71.5 0.1 copy.42
  71.6 0.9 all_to_all.16
  72.5 0.0 all-gather.2.cloned.1.call-update
  72.5 28.7 %psum.7 = f32[64]{0:T(128)S(1)} all-reduce(f32[64]{0:T(128)S(1)} %get-tuple-element.2), channel_id=1, replica_groups=mesh['feed'=32,'tm'=16] {'tm'}, use_global_device_ids=true, to_apply=%region_1.2 | all-reduce | flops 64 | bytes 512 | tf_op jit(solution)/shard_map/psum | solution.py:61
  101.2 0.1 dynamic-slice_maximum_fusion
  101.3 5.5 %all-gather.2.cloned.1.call-done = bf16[4,128,2048]{2,1,0:T(8,128)(2,1)} async-done(((bf16[4,8,2048]{2,1,0:T(8,128)(2,1)}), bf16[4,128,2048]{2,1,0:T(8,128)(2,1)}) %all-gather.2.cloned.1.call-update) | async-done | bytes 2097168 | tf_op jit(solution)/shard_map/all_gather | solution.py:68
  106.8 0.0 copy-start
  106.8 1.8 %slice_bitcast_fusion.1 = (bf16[2,128,2048]{2,1,0:T(8,128)(2,1)S(1)}, bf16[2,128,2048]{2,1,0:T(8,128)(2,1)S(1)}) fusion(bf16[2,2,128,2048]{3,2,1,0:T(8,128)(2,1)} %bitcast.38), kind=kLoop, calls=%fused_computation.24 | loop fusion | bytes 4194304 | tf_op jit(solution)/shard_map/squeeze | solution.py:31
  108.6 0.4 copy-done
  109.0 0.1 fusion.40
  109.1 0.1 fusion.37
  109.1 0.8 divide_convert_fusion
  109.9 1.5 %fusion.43 = (bf16[2,128,2048]{2,1,0:T(8,128)(2,1)}, bf16[2,128,2048]{2,1,0:T(8,128)(2,1)}) fusion(bf16[2,256,2048]{2,1,0:T(8,128)(2,1)S(1)} %divide_convert_fusion), kind=kLoop, calls=%fused_computation.53 | loop fusion | bytes 4194304 | tf_op jit(solution)/shard_map/slice | solution.py:72
  (5 shorter events, 0.1 us)
Async XLA Ops:
  7.2 99.6 %all-gather.2.cloned.1.call-start = ((), (), s32[]{:S(2)}) async-start(), calls=%async_computation.1 | async-start | bytes 2228224 | tf_op jit(solution)/shard_map/all_gather | solution.py:68
  8.4 14.3 %collective-permute-start = (bf16[64,6144]{1,0:T(8,128)(2,1)S(1)}, bf16[64,6144]{1,0:T(8,128)(2,1)}, u32[]{:S(2)}, u32[]{:S(2)}) collective-permute-start(bf16[64,6144]{1,0:T(8,128)(2,1)S(1)} %slice.29), channel_id=1, source_target_pairs={{0,1},{1,2},{2,3},{3,4},{4,5},{5,6},{6,7},{7,8},{8,9},{9,10},{10,1... | collective-permute-start | bytes 2359304 | tf_op jit(solution)/shard_map/ppermute | solution.py:12
  17.5 1.1 copy-start.3
  17.5 1.1 copy-start.4
  17.5 1.8 %copy-start.5 = (s32[64]{0:T(128)S(1)}, s32[64]{0:T(128)}, u32[]{:S(2)}) copy-start(s32[64]{0:T(128)} %param.7) | copy-start | bytes 772
  19.6 3.1 %copy-start.1 = (bf16[64,16384]{1,0:T(8,128)(2,1)S(1)}, bf16[64,16384]{1,0:T(8,128)(2,1)}, u32[]{:S(2)}) copy-start(bf16[64,16384]{1,0:T(8,128)(2,1)} %param.4) | copy-start | bytes 6291460
  39.6 1.6 %copy-start.2 = (bf16[8192,128]{1,0:T(8,128)(2,1)S(1)}, bf16[8192,128]{1,0:T(8,128)(2,1)}, u32[]{:S(2)}) copy-start(bf16[8192,128]{1,0:T(8,128)(2,1)} %fusion.9) | copy-start | bytes 6291460
  106.8 2.2 %copy-start = (bf16[4,128,2048]{2,1,0:T(8,128)(2,1)S(1)}, bf16[4,128,2048]{2,1,0:T(8,128)(2,1)}, u32[]{:S(2)}) copy-start(bf16[4,128,2048]{2,1,0:T(8,128)(2,1)} %all-gather.2.cloned.1.call-done) | copy-start | bytes 6291460
Sparse Core Ops, SparseCore 0:
  72.6 34.0 all-gather.1
where the time goes:
time: 119 us; the launch traced here: 118 us
  blocking collectives  55.5 us (47%)
  local copies, waits for them, and re-layouts  26.2 us (22%)
  between operations  14.3 us (12%)
  other arithmetic  6.98 us (6%)
  waiting for transfers between devices  6.2 us (5%)
  starting transfers between devices  5.43 us (5%)
  matrix products  3.61 us (3%)
    psum x1, blocking collectives, body(): counts_all = lax.psum(jnp.sum(good, axis=0), 'tm')  28.7 us
    all_to_all x1, blocking collectives, body(): lax.all_to_all(spectra, 'feed', split_axis=0, concat_axis=2, tiled=True)  26.8 us
    slice x1, local copies, waits for them, and re-layouts, body(): extended[:, t:t + spec_local, :]  8.57 us
    unnamed x20, local copies, waits for them, and re-layouts  5.95 us
    all_gather x1, waiting for transfers between devices, body(): every_spec = lax.all_gather(turned, 'tm', axis=1, tiled=True)  5.47 us
    ppermute x1, starting transfers between devices, shifted(): return lax.ppermute(block, axis, route)  5.39 us
    reshape x1, local copies, waits for them, and re-layouts, body(): jnp.concatenate([earlier, voltages], axis=1)  3.5 us
    dot_general x1, matrix products, body(): jnp.einsum('isk,kc->csi', frames, table, preferred_element_type=jnp.float32)  2.83 us
  transfers between devices with their start and end apart: 2, of which 2 were waited for; matrix products, arithmetic and copies ran while one was open for 7% of the time, Pallas kernels for 0%

commit v1 on v0

v1 whole, which is shorter than its diff:
```python
import functools
import math

import jax
import jax.numpy as jnp
from jax import lax
from jax.experimental import pallas as pl
from jax.experimental.pallas import tpu as pltpu
from jax.sharding import PartitionSpec as P

CHAN0 = 448
NF = 32
NT = 16
INPUTS = 64
FRAMES = 8
TAPS = 4
FRAME = 2048
COLS = 2048
HALF = COLS // 2
NCHAN = 4 * NF
MESH = pl.DeviceIdType.MESH
SINE = [(math.pi / 2) ** n / math.factorial(n) * (-1) ** (n // 2) for n in (1, 3, 5, 7, 9, 11)]

GATHER = {
    0: ("own", "all", "sib"),
    1: ("own", "all", "zed"),
    2: ("own", "all", "right"),
    3: ("own", "all", "left"),
    4: ("z", "all", "sib"),
    5: ("z", "all", "right"),
    6: ("z", "all", "left"),
    7: ("l", "all", "sib"),
    8: ("l", "lo", "right"),
    9: ("r", "all", "sib"),
    10: ("r", "hi", "left"),
    11: ("lz", "all", "sib"),
    12: ("lz", "lo", "right"),
    13: ("rz", "all", "sib"),
    14: ("rz", "hi", "left"),
    15: ("o", "lo", "sib"),
    16: ("o", "hi", "sib"),
    17: ("oz", "lo", "sib"),
    18: ("oz", "hi", "sib"),
}
EVENTS = len(GATHER)


def kernel(volt, coef, flags, order, out_re, out_im, frames, table, prod, halo_out, halo_in, rows,
           send_buf, recv_buf, count_buf, full, stage_re, stage_im,
           load_sem, halo_sem, turn_sem, count_sem, gather_send, gather_recv, own_sem, store_sem):
    f32 = jnp.float32
    bf16 = jnp.bfloat16
    feed = lax.axis_index("feed")
    tm = lax.axis_index("tm")

    barrier = pltpu.get_barrier_semaphore()

    def greet(axis, here, count):
        def one(step, carry):
            peer = lax.rem(here + step, count)
            pl.semaphore_signal(barrier, inc=1, device_id={axis: peer}, device_id_type=MESH)
            return carry

        lax.fori_loop(1, count, one, 0)

    loads = []
    for f in (7, 6, 5, 4, 3, 2, 1, 0):
        load = pltpu.make_async_copy(
            volt.at[:, pl.ds(f * FRAME, FRAME)], frames.at[pl.ds(f * INPUTS, INPUTS), :], load_sem.at[f]
        )
        load.start()
        loads.append(load)
    greet("tm", tm, NT)
    greet("feed", feed, NF)

    c_row = lax.broadcasted_iota(jnp.int32, (NCHAN, 2 * NF), 0)
    k_col = lax.broadcasted_iota(jnp.int32, (NCHAN, 2 * NF), 1)
    pick = k_col == 2 * (c_row & (NF - 1)) + (c_row >> 6)
    order_f = order[...].astype(f32)
    place = jnp.sum(jnp.where(pick, order_f, 0.0), axis=1, keepdims=True)
    chan_of = place.astype(jnp.int32)
    freq = jnp.broadcast_to(chan_of + CHAN0, (NCHAN, 128))
    lane = lax.broadcasted_iota(jnp.int32, (NCHAN, 128), 1)
    part = (lax.broadcasted_iota(jnp.int32, (NCHAN, 128), 0) >> 5) & 1
    phase0 = freq * lane + part * (FRAME // 4)
    phase_step = freq * 128
    scale = (TAPS * FRAME / 2.0) ** (-0.5)

    def table_block(a, phase):
        cols = pl.ds(pl.multiple_of(a * 128, 128), 128)
        dist = jnp.abs((phase & (FRAME - 1)) - FRAME // 2).astype(f32)
        z = dist * (4.0 / FRAME) - 1.0
        z2 = z * z
        trig = jnp.full_like(z, SINE[-1])
        for term in SINE[-2::-1]:
            trig = trig * z2 + term
        trig = trig * z
        for t in range(TAPS):
            table[pl.ds(t * NCHAN, NCHAN), cols] = (trig * (coef[pl.ds(t, 1), cols] * scale)).astype(bf16)
        return phase + phase_step

    lax.fori_loop(0, FRAME // 128, table_block, phase0)

    hot = (lax.broadcasted_iota(jnp.int32, (NCHAN, 2 * NF), 1) == chan_of).astype(bf16)
    nt = (((1,), (1,)), ((), ()))
    good = lax.dot_general(flags[...].astype(f32).astype(bf16), hot, nt, preferred_element_type=f32)
    local = jnp.sum(good, axis=0, keepdims=True)
    lane1 = lax.broadcasted_iota(jnp.int32, (1, NCHAN), 1)
    counts = [
        jnp.sum(jnp.where(lane1 == feed + kl * 2 * NF, local, 0.0), axis=1, keepdims=True) for kl in range(2)
    ]
    sub8 = lax.broadcasted_iota(jnp.int32, (8, 128), 0)
    count_buf[tm] = jnp.where(sub8 < 4, counts[0], counts[1])

    for load in loads[:4]:
        load.wait()
    prod[pl.ds(256, 256), :] = lax.dot_general(
        frames[pl.ds(256, 256), :], table[...], nt, preferred_element_type=f32
    )

    def term(f, t):
        return prod[pl.ds(f * INPUTS, INPUTS), pl.ds(t * NCHAN, NCHAN)]

    def partial(s):
        terms = [term(s - 3 + t, t) for t in range(TAPS) if 0 <= s - 3 + t < FRAMES]
        total = terms[0]
        for other in terms[1:]:
            total = total + other
        return total

    for s in range(3):
        halo_out[pl.ds(s * INPUTS, INPUTS), :] = partial(FRAMES + s)

    pl.semaphore_wait(barrier, NT - 1 + NF - 1)

    halo = pltpu.make_async_remote_copy(
        src_ref=halo_out, dst_ref=halo_in, send_sem=halo_sem.at[0], recv_sem=halo_sem.at[1],
        device_id={"tm": lax.rem(tm + 1, NT)}, device_id_type=MESH,
    )
    halo.start()

    def send_count(step, carry):
        pltpu.make_async_remote_copy(
            src_ref=count_buf.at[tm], dst_ref=count_buf.at[tm],
            send_sem=count_sem.at[0], recv_sem=count_sem.at[1],
            device_id={"tm": lax.rem(tm + step, NT)}, device_id_type=MESH,
        ).start()
        return carry

    lax.fori_loop(1, NT, send_count, 0)

    for load in loads[4:]:
        load.wait()
    prod[pl.ds(0, 256), :] = lax.dot_general(
        frames[pl.ds(0, 256), :], table[...], nt, preferred_element_type=f32
    )

    def turn(j):
        pair = []
        for s in (2 * j, 2 * j + 1):
            value = partial(s)
            if s < 3:
                value = value + jnp.where(tm > 0, halo_in[pl.ds(s * INPUTS, INPUTS), :], 0.0)
            pair.append(value * good[s : s + 1, :])
        turned = jnp.concatenate(pair, axis=0).T
        for q in range(4):
            rows[:, q * 4 + j, :] = turned[q * NF : (q + 1) * NF, :]

    turn(3)
    turn(2)
    halo.wait_recv()
    turn(1)
    turn(0)
    send_buf[...] = rows[...].astype(bf16)

    def send_rows(step, carry):
        peer = lax.rem(feed + step, NF)
        pltpu.make_async_remote_copy(
            src_ref=send_buf.at[peer], dst_ref=recv_buf.at[feed],
            send_sem=turn_sem.at[0], recv_sem=turn_sem.at[1],
            device_id={"feed": peer}, device_id_type=MESH,
        ).start()
        return carry

    lax.fori_loop(1, NF, send_rows, 0)
    own = pltpu.make_async_copy(send_buf.at[feed], recv_buf.at[feed], own_sem)
    own.start()
    own.wait()
    others = recv_buf.at[pl.ds(0, NF - 1)]
    pltpu.make_async_copy(others, others, turn_sem.at[1]).wait()

    low = lax.broadcasted_iota(jnp.int32, (16, 128), 1) < INPUTS
    for g in range(NF // 2):
        one = recv_buf[2 * g].astype(f32)
        two = recv_buf[2 * g + 1].astype(f32)
        first = jnp.where(low, one, pltpu.roll(two, INPUTS, 1))
        second = jnp.where(low, pltpu.roll(one, INPUTS, 1), two)
        for kl in range(2):
            full[kl, tm, :, pl.ds(g * 128, 128)] = jnp.concatenate(
                [first[kl * 8 : kl * 8 + 8], second[kl * 8 : kl * 8 + 8]], axis=0
            ).astype(bf16)

    x, zed, core = tm // 4, lax.rem(tm // 2, 2), lax.rem(tm, 2)

    def at(dx, dz, dc):
        return lax.rem(x + dx, 4) * 4 + lax.rem(zed + dz, 2) * 2 + lax.rem(core + dc, 2)

    targets = {"sib": at(0, 0, 1), "zed": at(0, 1, 0), "right": at(1, 0, 0), "left": at(3, 0, 0)}
    blocks = {"own": (0, 0), "z": (0, 1), "l": (3, 0), "r": (1, 0), "lz": (3, 1), "rz": (1, 1), "o": (2, 0), "oz": (2, 1)}
    moves = {"sib": (0, 0, 1), "zed": (0, 1, 0), "right": (3, 0, 0), "left": (1, 0, 0)}
    lanes = {"all": pl.ds(0, COLS), "lo": pl.ds(0, HALF), "hi": pl.ds(HALF, HALF)}

    def view(kl, index, which):
        return full.at[kl, index, :, lanes[which]]

    def send(kl, event):
        block, which, target = GATHER[event]
        ref = view(kl, at(*blocks[block], 0), which)
        copy = pltpu.make_async_remote_copy(
            src_ref=ref, dst_ref=ref,
            send_sem=gather_send.at[kl, event], recv_sem=gather_recv.at[kl, event],
            device_id={"tm": targets[target]}, device_id_type=MESH,
        )
        copy.start()

    def arrived(kl, event):
        block, which, target = GATHER[event]
        dx, dz = blocks[block]
        mx, mz, mc = moves[target]
        ref = view(kl, at((dx + mx) % 4, (dz + mz) % 2, mc), which)
        pltpu.make_async_copy(ref, ref, gather_recv.at[kl, event]).wait()

    def sent(kl, event):
        block, which, _ = GATHER[event]
        ref = view(kl, at(*blocks[block], 0), which)
        pltpu.make_async_copy(ref, ref, gather_send.at[kl, event]).wait()

    def relay(kl, event, *following):
        arrived(kl, event)
        for after in following:
            send(kl, after)

    for kl in range(2):
        for event in (2, 3, 1, 0):
            send(kl, event)
    for kl in range(2):
        relay(kl, 1, 5, 6, 4)
        relay(kl, 2, 8, 7)
        relay(kl, 3, 10, 9)
    for kl in range(2):
        relay(kl, 5, 12, 11)
        relay(kl, 6, 14, 13)

    every = count_buf.at[pl.ds(0, NT - 1)]
    pltpu.make_async_copy(every, every, count_sem.at[1]).wait()
    total = jnp.sum(count_buf[...], axis=0)
    inverse = 1.0 / jnp.maximum(total, 1.0)

    mine = pl.ds(pl.multiple_of(tm * 128, 128), 128)
    stores = []

    def correlate(kl):
        left = full[kl, :, :, mine].reshape(32, 8, 128).astype(f32)
        swapped = jnp.concatenate([left[:, 4:], -left[:, :4]], axis=1)
        both = jnp.concatenate([left.reshape(256, 128).T, swapped.reshape(256, 128).T], axis=0).astype(bf16)
        factor = inverse[4 * kl : 4 * kl + 1, 0:1]

        def column(n, carry):
            cols = pl.ds(pl.multiple_of(n * 512, 512), 512)
            right = full[kl, :, :, cols].reshape(256, 512)
            result = jnp.dot(both, right, preferred_element_type=f32) * factor
            stage_re[kl, :, cols] = result[:128].astype(bf16)
            stage_im[kl, :, cols] = result[128:].astype(bf16)
            return carry

        lax.fori_loop(0, COLS // 512, column, 0)
        for n, (stage, out) in enumerate(((stage_re, out_re), (stage_im, out_im))):
            store = pltpu.make_async_copy(stage.at[kl], out.at[kl], store_sem.at[kl, n])
            store.start()
            stores.append(store)

    for kl in range(2):
        relay(kl, 8, 15)
        relay(kl, 10, 16)
        relay(kl, 12, 17)
        relay(kl, 14, 18)
        for event in (0, 4, 7, 9, 11, 13, 15, 16, 17, 18):
            arrived(kl, event)
        correlate(kl)

    halo.wait_send()
    pltpu.make_async_copy(every, every, count_sem.at[0]).wait()
    gone = send_buf.at[pl.ds(0, NF - 1)]
    pltpu.make_async_copy(gone, gone, turn_sem.at[0]).wait()
    for kl in range(2):
        for event in range(EVENTS):
            sent(kl, event)
    for store in stores:
        store.wait()


def body(voltages, pfb_coeffs, flags, channel_order):
    vmem = pl.BlockSpec(memory_space=pltpu.VMEM)
    anywhere = pl.BlockSpec(memory_space=pl.ANY)
    out = jax.ShapeDtypeStruct((2, 128, COLS), jnp.bfloat16)
    dma = pltpu.SemaphoreType.DMA
    return pl.pallas_call(
        kernel,
        out_shape=(out, out),
        in_specs=[anywhere, vmem, vmem, vmem],
        out_specs=(anywhere, anywhere),
        scratch_shapes=[
            pltpu.VMEM((FRAMES * INPUTS, FRAME), jnp.bfloat16),
            pltpu.VMEM((TAPS * NCHAN, FRAME), jnp.bfloat16),
            pltpu.VMEM((FRAMES * INPUTS, TAPS * NCHAN), jnp.float32),
            pltpu.VMEM((3 * INPUTS, NCHAN), jnp.float32),
            pltpu.VMEM((3 * INPUTS, NCHAN), jnp.float32),
            pltpu.VMEM((NF, 16, 128), jnp.float32),
            pltpu.VMEM((NF, 16, 128), jnp.bfloat16),
            pltpu.VMEM((NF, 16, 128), jnp.bfloat16),
            pltpu.VMEM((NT, 8, 128), jnp.float32),
            pltpu.VMEM((2, NT, 16, COLS), jnp.bfloat16),
            pltpu.VMEM((2, 128, COLS), jnp.bfloat16),
            pltpu.VMEM((2, 128, COLS), jnp.bfloat16),
            dma((FRAMES,)),
            dma((2,)),
            dma((2,)),
            dma((2,)),
            dma((2, EVENTS)),
            dma((2, EVENTS)),
            dma,
            dma((2, 2)),
        ],
        compiler_params=pltpu.CompilerParams(
            collective_id=0, has_side_effects=True, vmem_limit_bytes=32 * 1024 * 1024
        ),
        name="channelize_correlate",
    )(voltages, pfb_coeffs, flags, channel_order.reshape(1, -1))


def solution(mesh):
    return jax.shard_map(
        body,
        mesh=mesh,
        in_specs=(P("feed", "tm"), P(), P("tm", None), P()),
        out_specs=(P("feed", "tm", None), P("feed", "tm", None)),
        check_vma=False,
    )
```

time: 119 us -> 47.8 us (0.40)
  blocking collectives: 55.5 us -> 0 us
  Pallas kernels: 0 us -> 41.3 us
  local copies, waits for them, and re-layouts: 26.2 us -> 5.62 us
  between operations: 14.3 us -> 0.65 us
  other arithmetic: 6.98 us -> 0 us
  waiting for transfers between devices: 6.2 us -> 0 us
  starting transfers between devices: 5.43 us -> 0 us
  matrix products: 3.61 us -> 0 us
    pallas_call x0 -> x1, Pallas kernels: none -> 41.3 us  [body(): pl.pallas_call(kernel, out_shape=(out, out), in_specs=[anywhere, vmem, vm...]
    psum x1 -> x0, blocking collectives: 28.7 us -> none  [body(): counts_all = lax.psum(jnp.sum(good, axis=0), 'tm')]
    all_to_all x1 -> x0, blocking collectives: 26.8 us -> none  [body(): lax.all_to_all(spectra, 'feed', split_axis=0, concat_axis=2, tiled=True)]
    slice x3 -> x0, local copies, waits for them, and re-layouts: 11.2 us -> none  [the longest x1 8.57 us: body(): extended[:, t:t + spec_local, :]]
    all_gather x1 -> x0, waiting for transfers between devices: 5.47 us -> none  [body(): every_spec = lax.all_gather(turned, 'tm', axis=1, tiled=True)]
    ppermute x1 -> x0, starting transfers between devices: 5.39 us -> none  [shifted(): return lax.ppermute(block, axis, route)]
    dot_general x2 -> x0, matrix products: 3.61 us -> none  [the longest x1 2.83 us: body(): jnp.einsum('isk,kc->csi', frames, table, preferred_element_type=jnp.float32)]
    reshape x1 -> x0, local copies, waits for them, and re-layouts: 3.5 us -> none  [body(): jnp.concatenate([earlier, voltages], axis=1)]
  transfers between devices with their start and end apart: 2 -> 0, of which waited for: 2 -> 0; matrix products, arithmetic and copies ran while one was open for 7% -> 0% of each run, Pallas kernels for 0% -> 0%
where the time goes in v1:
time: 47.8 us; the launch traced here: 47.6 us
  Pallas kernels  41.3 us (86%)
  local copies, waits for them, and re-layouts  5.62 us (12%)
  between operations  0.65 us (1%)
    pallas_call x1, Pallas kernels, body(): pl.pallas_call(kernel, out_shape=(out, out), in_specs=[anywhere, vmem, vm...  41.3 us
    unnamed x10, local copies, waits for them, and re-layouts  5.62 us

profile of v1, /device:TPU:1, one launch (start us, length us, event | category | flops | bytes accessed | tf_op | source)
XLA Modules:
  0.0 47.6 jit_solution(3103021778560935702)
XLA Ops:
  0.6 0.0 copy-start
  0.6 1.6 %copy-done = bf16[64,16384]{1,0:T(8,128)(2,1)S(1)} copy-done((bf16[64,16384]{1,0:T(8,128)(2,1)S(1)}, bf16[64,16384]{1,0:T(8,128)(2,1)}, u32[]{:S(2)}) %copy-start) | copy-done | bytes 2097176
  2.2 0.0 copy-start.1
  2.2 0.8 %copy-done.1 = f32[4,2048]{1,0:T(4,128)S(1)} copy-done((f32[4,2048]{1,0:T(4,128)S(1)}, f32[4,2048]{1,0:T(4,128)}, u32[]{:S(2)}) %copy-start.1) | copy-done | bytes 32792
  3.0 0.0 copy-start.2
  3.0 0.7 %copy-done.2 = s32[8,64]{1,0:T(8,128)S(1)} copy-done((s32[8,64]{1,0:T(8,128)S(1)}, s32[8,64]{1,0:T(8,128)}, u32[]{:S(2)}) %copy-start.2) | copy-done | bytes 2072
  3.7 0.0 copy-start.3
  3.7 0.7 %copy-done.3 = s32[64]{0:T(128)S(1)} copy-done((s32[64]{0:T(128)S(1)}, s32[64]{0:T(128)}, u32[]{:S(2)}) %copy-start.3) | copy-done | bytes 280
  4.3 41.3 %channelize_correlate.1 = (bf16[2,128,2048]{2,1,0:T(8,128)(2,1)S(1)}, bf16[2,128,2048]{2,1,0:T(8,128)(2,1)S(1)}) custom-call(bf16[64,16384]{1,0:T(8,128)(2,1)S(1)} %copy-done, f32[4,2048]{1,0:T(4,128)S(1)} %copy-done.1, s32[8,64]{1,0:T(8,128)S(1)} %copy-done.2, s32[1,64]{1,0:T(1,128)S(1)} %bitcast.1), custom_call_target="tpu_custom_call" | custom-call | tf_op jit(solution)/shard_map/channelize_correlate/pallas_call | solution.py:307
  45.6 1.0 %copy.8 = bf16[2,128,2048]{2,1,0:T(8,128)(2,1)} copy(bf16[2,128,2048]{2,1,0:T(8,128)(2,1)S(1)} %get-tuple-element.4) | data formatting | bytes 2097152
  46.6 1.0 %copy.9 = bf16[2,128,2048]{2,1,0:T(8,128)(2,1)} copy(bf16[2,128,2048]{2,1,0:T(8,128)(2,1)S(1)} %get-tuple-element.5) | data formatting | bytes 2097152
Async XLA Ops:
  0.6 1.6 %copy-start = (bf16[64,16384]{1,0:T(8,128)(2,1)S(1)}, bf16[64,16384]{1,0:T(8,128)(2,1)}, u32[]{:S(2)}) copy-start(bf16[64,16384]{1,0:T(8,128)(2,1)} %volt.1) | copy-start | bytes 6291460
  2.2 0.8 %copy-start.1 = (f32[4,2048]{1,0:T(4,128)S(1)}, f32[4,2048]{1,0:T(4,128)}, u32[]{:S(2)}) copy-start(f32[4,2048]{1,0:T(4,128)} %coef.1) | copy-start | bytes 98308
  3.0 0.7 %copy-start.2 = (s32[8,64]{1,0:T(8,128)S(1)}, s32[8,64]{1,0:T(8,128)}, u32[]{:S(2)}) copy-start(s32[8,64]{1,0:T(8,128)} %flags.1) | copy-start | bytes 6148
  3.7 0.7 %copy-start.3 = (s32[64]{0:T(128)S(1)}, s32[64]{0:T(128)}, u32[]{:S(2)}) copy-start(s32[64]{0:T(128)} %param.7) | copy-start | bytes 772

commit v2 on v1

v2 whole, which is shorter than its diff:
```python
import functools
import math

import jax
import jax.numpy as jnp
from jax import lax
from jax.experimental import pallas as pl
from jax.experimental.pallas import tpu as pltpu
from jax.sharding import PartitionSpec as P

CHAN0 = 448
NF = 32
NT = 16
INPUTS = 64
FRAMES = 8
TAPS = 4
FRAME = 2048
COLS = 2048
HALF = COLS // 2
WIDE = 512
NCHAN = 4 * NF
MESH = pl.DeviceIdType.MESH
SINE = [(math.pi / 2) ** n / math.factorial(n) * (-1) ** (n // 2) for n in (1, 3, 5, 7, 9, 11)]

GATHER = {
    0: ("own", "all", "sib"),
    1: ("own", "all", "zed"),
    2: ("own", "all", "right"),
    3: ("own", "all", "left"),
    4: ("z", "all", "sib"),
    5: ("z", "all", "right"),
    6: ("z", "all", "left"),
    7: ("l", "all", "sib"),
    8: ("l", "lo", "right"),
    9: ("r", "all", "sib"),
    10: ("r", "hi", "left"),
    11: ("lz", "all", "sib"),
    12: ("lz", "lo", "right"),
    13: ("rz", "all", "sib"),
    14: ("rz", "hi", "left"),
    15: ("o", "lo", "sib"),
    16: ("o", "hi", "sib"),
    17: ("oz", "lo", "sib"),
    18: ("oz", "hi", "sib"),
}
EVENTS = len(GATHER)

FAR = sorted(
    ((dz, dy) for dz in range(4) for dy in range(8) if dz or dy),
    key=lambda step: -(2 * min(step[0], 4 - step[0]) + min(step[1], 8 - step[1])),
)


def kernel(volt, coef_hbm, flags_hbm, order_hbm, full, count_buf, coef, flags, order, frames, table, prod,
           rows, send_buf, recv_buf, next_buf, prev_buf,
           small_sem, load_sem, next_sem, turn_sem, count_sem, gather_send, gather_recv, own_sem):
    f32 = jnp.float32
    bf16 = jnp.bfloat16
    feed = lax.axis_index("feed")
    tm = lax.axis_index("tm")

    z_hi, y = feed // 8, lax.rem(feed, 8)
    after, before = lax.rem(tm + 1, NT), lax.rem(tm + NT - 1, NT)

    def feed_at(dz, dy):
        return lax.rem(z_hi + dz, 4) * 8 + lax.rem(y + dy, 8)

    barrier = pltpu.get_barrier_semaphore()

    def greet(feed_to, tm_to):
        pl.semaphore_signal(barrier, inc=1, device_id={"feed": feed_to, "tm": tm_to}, device_id_type=MESH)

    smalls = [
        pltpu.make_async_copy(src, dst, small_sem.at[n])
        for n, (src, dst) in enumerate(((order_hbm, order), (coef_hbm, coef), (flags_hbm, flags)))
    ]
    for small in smalls:
        small.start()
    loads = []
    for f in (7, 6, 5, 4, 3, 2, 1, 0):
        load = pltpu.make_async_copy(
            volt.at[:, pl.ds(f * FRAME, FRAME)], frames.at[pl.ds(f * INPUTS, INPUTS), :], load_sem.at[f]
        )
        load.start()
        loads.append(load)
    for step in FAR:
        greet(feed_at(*step), before)
        greet(feed_at(*step), tm)
    for step in range(1, NT):
        greet(feed, lax.rem(tm + step, NT))

    for small in smalls:
        small.wait()

    c_row = lax.broadcasted_iota(jnp.int32, (NCHAN, 2 * NF), 0)
    k_col = lax.broadcasted_iota(jnp.int32, (NCHAN, 2 * NF), 1)
    pick = k_col == 2 * (c_row & (NF - 1)) + (c_row >> 6)
    order_f = order[...].astype(f32)
    place = jnp.sum(jnp.where(pick, order_f, 0.0), axis=1, keepdims=True)
    chan_of = place.astype(jnp.int32)
    freq = jnp.broadcast_to(chan_of + CHAN0, (NCHAN, 128))
    lane = lax.broadcasted_iota(jnp.int32, (NCHAN, 128), 1)
    part = (lax.broadcasted_iota(jnp.int32, (NCHAN, 128), 0) >> 5) & 1
    phase0 = freq * lane + part * (FRAME // 4)
    phase_step = freq * 128
    scale = (TAPS * FRAME / 2.0) ** (-0.5)

    def table_block(a, phase):
        cols = pl.ds(pl.multiple_of(a * 128, 128), 128)
        dist = jnp.abs((phase & (FRAME - 1)) - FRAME // 2).astype(f32)
        z = dist * (4.0 / FRAME) - 1.0
        z2 = z * z
        trig = jnp.full_like(z, SINE[-1])
        for term in SINE[-2::-1]:
            trig = trig * z2 + term
        trig = trig * z
        for t in range(TAPS):
            table[pl.ds(t * NCHAN, NCHAN), cols] = (trig * (coef[pl.ds(t, 1), cols] * scale)).astype(bf16)
        return phase + phase_step

    lax.fori_loop(0, FRAME // 128, table_block, phase0)

    hot = (lax.broadcasted_iota(jnp.int32, (NCHAN, 2 * NF), 1) == chan_of).astype(bf16)
    nt = (((1,), (1,)), ((), ()))
    good = lax.dot_general(flags[...].astype(f32).astype(bf16), hot, nt, preferred_element_type=f32)
    local = jnp.sum(good, axis=0, keepdims=True)
    lane1 = lax.broadcasted_iota(jnp.int32, (1, NCHAN), 1)
    counts = [
        jnp.sum(jnp.where(lane1 == feed + kl * 2 * NF, local, 0.0), axis=1, keepdims=True) for kl in range(2)
    ]
    sub8 = lax.broadcasted_iota(jnp.int32, (8, 128), 0)
    count_buf[tm] = jnp.where(sub8 < 4, counts[0], counts[1])

    for load in loads:
        load.wait()
    prod[...] = lax.dot_general(frames[...], table[...], nt, preferred_element_type=f32)

    def term(f, t):
        return prod[pl.ds(f * INPUTS, INPUTS), pl.ds(t * NCHAN, NCHAN)]

    def partial(s):
        terms = [term(s - 3 + t, t) for t in range(TAPS) if 0 <= s - 3 + t < FRAMES]
        total = terms[0]
        for other in terms[1:]:
            total = total + other
        return total

    for j in range(2):
        last = partial(FRAMES + 2 * j + 1) if j == 0 else jnp.zeros((INPUTS, NCHAN), f32)
        turned = jnp.concatenate([partial(FRAMES + 2 * j), last], axis=0).T
        for q in range(4):
            next_buf[:, (q // 2) * 4 + (q % 2) * 2 + j, :] = turned[q * NF : (q + 1) * NF, :]
    for j in range(4):
        turned = jnp.concatenate([partial(2 * j), partial(2 * j + 1)], axis=0).T
        for q in range(4):
            rows[:, (q // 2) * 8 + (j // 2) * 4 + (q % 2) * 2 + j % 2, :] = turned[q * NF : (q + 1) * NF, :]
    send_buf[...] = rows[...].astype(bf16)

    pl.semaphore_wait(barrier, 2 * (NF - 1) + NT - 1)

    def send_next(peer):
        pltpu.make_async_remote_copy(
            src_ref=next_buf.at[peer], dst_ref=prev_buf.at[feed],
            send_sem=next_sem.at[0], recv_sem=next_sem.at[1],
            device_id={"feed": peer, "tm": after}, device_id_type=MESH,
        ).start()

    for step in FAR:
        peer = feed_at(*step)
        send_next(peer)
        pltpu.make_async_remote_copy(
            src_ref=send_buf.at[peer], dst_ref=recv_buf.at[feed],
            send_sem=turn_sem.at[0], recv_sem=turn_sem.at[1],
            device_id={"feed": peer, "tm": tm}, device_id_type=MESH,
        ).start()
    send_next(feed)
    own = pltpu.make_async_copy(send_buf.at[feed], recv_buf.at[feed], own_sem.at[0])
    own.start()

    def send_count(step, carry):
        pltpu.make_async_remote_copy(
            src_ref=count_buf.at[tm], dst_ref=count_buf.at[tm],
            send_sem=count_sem.at[0], recv_sem=count_sem.at[1],
            device_id={"tm": lax.rem(tm + step, NT)}, device_id_type=MESH,
        ).start()
        return carry

    lax.fori_loop(1, NT, send_count, 0)

    row = lax.broadcasted_iota(jnp.int32, (32, FRAMES), 0)
    spec = (row & 1) * 2 + ((row >> 2) & 1) * 4 + (row >> 4)
    match = (spec == lax.broadcasted_iota(jnp.int32, (32, FRAMES), 1)).astype(bf16)
    every_flag = jnp.dot(match, good.astype(bf16), preferred_element_type=f32)
    row = lax.broadcasted_iota(jnp.int32, (32, NCHAN), 0)
    mine = lax.broadcasted_iota(jnp.int32, (32, NCHAN), 1) == feed + ((row >> 3) & 1) * 2 * NF
    clean = jnp.sum(jnp.where(mine, every_flag, 0.0), axis=1, keepdims=True)

    own.wait()
    others = recv_buf.at[pl.ds(0, NF - 1)]
    pltpu.make_async_copy(others, others, turn_sem.at[1]).wait()
    pltpu.make_async_copy(prev_buf, prev_buf, next_sem.at[1]).wait()

    low = lax.broadcasted_iota(jnp.int32, (16, 128), 1) < INPUTS
    top = jnp.logical_and(lax.broadcasted_iota(jnp.int32, (8, 128), 0) < 4, tm > 0)

    def received(f):
        prev = prev_buf[f]
        both = jnp.concatenate([jnp.where(top, prev, 0.0), jnp.where(top, pltpu.roll(prev, 4, 0), 0.0)], axis=0)
        return recv_buf[f].astype(f32) + both

    for g in range(NF // 2):
        one = received(2 * g)
        two = received(2 * g + 1)
        first = jnp.where(low, one, pltpu.roll(two, INPUTS, 1)) * clean[:16]
        second = jnp.where(low, pltpu.roll(one, INPUTS, 1), two) * clean[16:]
        for kl in range(2):
            block = jnp.concatenate([first[kl * 8 : kl * 8 + 8], second[kl * 8 : kl * 8 + 8]], axis=0)
            full[kl, tm, :, pl.ds(g * 128, 128)] = block.astype(bf16)

    x, zed, core = tm // 4, lax.rem(tm // 2, 2), lax.rem(tm, 2)

    def at(dx, dz, dc):
        return lax.rem(x + dx, 4) * 4 + lax.rem(zed + dz, 2) * 2 + lax.rem(core + dc, 2)

    targets = {"sib": at(0, 0, 1), "zed": at(0, 1, 0), "right": at(1, 0, 0), "left": at(3, 0, 0)}
    blocks = {"own": (0, 0), "z": (0, 1), "l": (3, 0), "r": (1, 0), "lz": (3, 1), "rz": (1, 1), "o": (2, 0), "oz": (2, 1)}
    moves = {"sib": (0, 0, 1), "zed": (0, 1, 0), "right": (3, 0, 0), "left": (1, 0, 0)}
    lanes = {"all": pl.ds(0, COLS), "lo": pl.ds(0, HALF), "hi": pl.ds(HALF, HALF)}

    def view(kl, index, which):
        return full.at[kl, index, :, lanes[which]]

    def send(kl, event):
        block, which, target = GATHER[event]
        ref = view(kl, at(*blocks[block], 0), which)
        copy = pltpu.make_async_remote_copy(
            src_ref=ref, dst_ref=ref,
            send_sem=gather_send.at[kl, event], recv_sem=gather_recv.at[kl, event],
            device_id={"tm": targets[target]}, device_id_type=MESH,
        )
        copy.start()

    def arrived(kl, event):
        block, which, target = GATHER[event]
        dx, dz = blocks[block]
        mx, mz, mc = moves[target]
        ref = view(kl, at((dx + mx) % 4, (dz + mz) % 2, mc), which)
        pltpu.make_async_copy(ref, ref, gather_recv.at[kl, event]).wait()

    def sent(kl, event):
        block, which, _ = GATHER[event]
        ref = view(kl, at(*blocks[block], 0), which)
        pltpu.make_async_copy(ref, ref, gather_send.at[kl, event]).wait()

    def relay(kl, event, *following):
        arrived(kl, event)
        for after in following:
            send(kl, after)

    for kl in range(2):
        for event in (2, 3, 1, 0):
            send(kl, event)
    for kl in range(2):
        relay(kl, 1, 5, 6, 4)
        relay(kl, 2, 8, 7)
        relay(kl, 3, 10, 9)
    for kl in range(2):
        relay(kl, 5, 12, 11)
        relay(kl, 6, 14, 13)

    for kl in range(2):
        relay(kl, 8, 15)
        relay(kl, 10, 16)
        relay(kl, 12, 17)
        relay(kl, 14, 18)
    every = count_buf.at[pl.ds(0, NT - 1)]
    pltpu.make_async_copy(every, every, count_sem.at[1]).wait()
    for kl in range(2):
        for event in (0, 4, 7, 9, 11, 13, 15, 16, 17, 18):
            arrived(kl, event)
    pltpu.make_async_copy(every, every, count_sem.at[0]).wait()
    gone = send_buf.at[pl.ds(0, NF - 1)]
    pltpu.make_async_copy(gone, gone, turn_sem.at[0]).wait()
    pltpu.make_async_copy(next_buf, next_buf, next_sem.at[0]).wait()
    for kl in range(2):
        for event in range(EVENTS):
            sent(kl, event)


def correlate(full, count_buf, out_re, out_im, stage_re, stage_im, store_sem):
    f32 = jnp.float32
    bf16 = jnp.bfloat16
    tm = lax.axis_index("tm")
    inverse = 1.0 / jnp.maximum(jnp.sum(count_buf[...], axis=0), 1.0)
    mine = pl.ds(pl.multiple_of(tm * 128, 128), 128)
    odd = (lax.broadcasted_iota(jnp.int32, (256, 128), 0) & 2) > 0
    stores = []
    for kl in range(2):
        left = full[kl, :, :, mine].reshape(256, 128).astype(f32)
        swapped = jnp.where(odd, -pltpu.roll(left, 2, 0), pltpu.roll(left, 254, 0))
        both = jnp.concatenate([left.T, swapped.T], axis=0).astype(bf16)
        factor = inverse[4 * kl : 4 * kl + 1, 0:1]
        for n in range(COLS // WIDE):
            cols = pl.ds(n * WIDE, WIDE)
            right = full[kl, :, :, cols].reshape(256, WIDE)
            result = jnp.dot(both, right, preferred_element_type=f32) * factor
            stage_re[kl, :, cols] = result[:128].astype(bf16)
            stage_im[kl, :, cols] = result[128:].astype(bf16)
            for part, (stage, out) in enumerate(((stage_re, out_re), (stage_im, out_im))):
                store = pltpu.make_async_copy(stage.at[kl, :, cols], out.at[kl, :, cols], store_sem.at[kl, n, part])
                store.start()
                stores.append(store)
    for store in stores:
        store.wait()


def body(voltages, pfb_coeffs, flags, channel_order):
    hbm = pl.BlockSpec(memory_space=pltpu.HBM)
    vmem = pl.BlockSpec(memory_space=pltpu.VMEM)
    bf16 = jnp.bfloat16
    f32 = jnp.float32
    dma = pltpu.SemaphoreType.DMA
    args = (voltages, pfb_coeffs, flags, channel_order.reshape(1, -1))
    full, counts = pl.pallas_call(
        kernel,
        out_shape=(jax.ShapeDtypeStruct((2, NT, 16, COLS), bf16), jax.ShapeDtypeStruct((NT, 8, 128), f32)),
        in_specs=[hbm] * 4,
        out_specs=(vmem, vmem),
        scratch_shapes=[
            pltpu.VMEM((TAPS, FRAME), f32),
            pltpu.VMEM((FRAMES, 2 * NF), jnp.int32),
            pltpu.VMEM((1, 2 * NF), jnp.int32),
            pltpu.VMEM((FRAMES * INPUTS, FRAME), bf16),
            pltpu.VMEM((TAPS * NCHAN, FRAME), bf16),
            pltpu.VMEM((FRAMES * INPUTS, TAPS * NCHAN), f32),
            pltpu.VMEM((NF, 16, 128), f32),
            pltpu.VMEM((NF, 16, 128), bf16),
            pltpu.VMEM((NF, 16, 128), bf16),
            pltpu.VMEM((NF, 8, 128), f32),
            pltpu.VMEM((NF, 8, 128), f32),
            dma((3,)),
            dma((FRAMES,)),
            dma((2,)),
            dma((2,)),
            dma((2,)),
            dma((2, EVENTS)),
            dma((2, EVENTS)),
            dma((1,)),
        ],
        compiler_params=pltpu.CompilerParams(
            collective_id=0, has_side_effects=True, vmem_limit_bytes=24 * 1024 * 1024
        ),
        name="channelize_gather",
    )(*(pltpu.with_memory_space_constraint(a, pltpu.HBM) for a in args))
    out = jax.ShapeDtypeStruct((2, 128, COLS), bf16)
    return pl.pallas_call(
        correlate,
        out_shape=(out, out),
        in_specs=[vmem, vmem],
        out_specs=(hbm, hbm),
        scratch_shapes=[
            pltpu.VMEM((2, 128, COLS), bf16),
            pltpu.VMEM((2, 128, COLS), bf16),
            dma((2, COLS // WIDE, 2)),
        ],
        compiler_params=pltpu.CompilerParams(vmem_limit_bytes=24 * 1024 * 1024),
        name="correlate",
    )(full, counts)


def solution(mesh):
    return jax.shard_map(
        body,
        mesh=mesh,
        in_specs=(P("feed", "tm"), P(), P("tm", None), P()),
        out_specs=(P("feed", "tm", None), P("feed", "tm", None)),
        check_vma=False,
    )
```

time: 47.8 us -> 43.3 us (0.906)
  local copies, waits for them, and re-layouts: 5.62 us -> 0 us
  Pallas kernels: 41.3 us -> 42.5 us
    unnamed x10 -> x0, local copies, waits for them, and re-layouts: 5.62 us -> none
    pallas_call x1 -> x2, Pallas kernels: 41.3 us -> 42.5 us  [the longest x1 40.8 us: body(): pl.pallas_call(kernel, out_shape=(jax.ShapeDtypeStruct((2, NT, 16, COLS),...]
where the time goes in v2:
time: 43.3 us; the launch traced here: 43.2 us
  Pallas kernels  42.5 us (98%)
  between operations  0.64 us (1%)
    pallas_call x1, Pallas kernels, body(): pl.pallas_call(kernel, out_shape=(jax.ShapeDtypeStruct((2, NT, 16, COLS),...  40.8 us
    pallas_call x1, Pallas kernels, body(): pl.pallas_call(correlate, out_shape=(out, out), in_specs=[vmem, vmem], ou...  1.7 us

profile of v2, /device:TPU:1, one launch (start us, length us, event | category | flops | bytes accessed | tf_op | source)
XLA Modules:
  0.0 43.2 jit_solution(7761308637593300046)
XLA Ops:
  0.6 40.8 %channelize_gather.1 = (bf16[2,16,16,2048]{3,2,1,0:T(8,128)(2,1)S(1)}, f32[16,8,128]{2,1,0:T(8,128)S(1)}) custom-call(bf16[64,16384]{1,0:T(8,128)(2,1)} %volt.1, f32[4,2048]{1,0:T(4,128)} %coef_hbm.1, s32[8,64]{1,0:T(8,128)} %flags_hbm.1, s32[1,64]{1,0:T(1,128)} %bitcast.1), custom_call_target="tpu_custom_call" | custom-call | tf_op jit(solution)/shard_map/channelize_gather/pallas_call | solution.py:324
  41.5 1.7 %correlate.1 = (bf16[2,128,2048]{2,1,0:T(8,128)(2,1)}, bf16[2,128,2048]{2,1,0:T(8,128)(2,1)}) custom-call(bf16[2,16,16,2048]{3,2,1,0:T(8,128)(2,1)S(1)} %get-tuple-element.4.full, f32[16,8,128]{2,1,0:T(8,128)S(1)} %get-tuple-element.5.count_buf), custom_call_target="tpu_custom_call" | custom-call | tf_op jit(solution)/shard_map/correlate/pallas_call | solution.py:356

commit v3 on v2

--- a/solution.py
+++ b/solution.py
@@ -22,28 +22,34 @@
 MESH = pl.DeviceIdType.MESH
 SINE = [(math.pi / 2) ** n / math.factorial(n) * (-1) ** (n // 2) for n in (1, 3, 5, 7, 9, 11)]
 
+BOTH = (0, 1)
 GATHER = {
-    0: ("own", "all", "sib"),
-    1: ("own", "all", "zed"),
-    2: ("own", "all", "right"),
-    3: ("own", "all", "left"),
-    4: ("z", "all", "sib"),
-    5: ("z", "all", "right"),
-    6: ("z", "all", "left"),
-    7: ("l", "all", "sib"),
-    8: ("l", "lo", "right"),
-    9: ("r", "all", "sib"),
-    10: ("r", "hi", "left"),
-    11: ("lz", "all", "sib"),
-    12: ("lz", "lo", "right"),
-    13: ("rz", "all", "sib"),
-    14: ("rz", "hi", "left"),
-    15: ("o", "lo", "sib"),
-    16: ("o", "hi", "sib"),
-    17: ("oz", "lo", "sib"),
-    18: ("oz", "hi", "sib"),
+    "own0z": ("own", (0,), "all", "zed", ()),
+    "own1r": ("own", (1,), "all", "right", ()),
+    "own1l": ("own", (1,), "all", "left", ()),
+    "own1o": ("own", (1,), "all", "over", ()),
+    "own1z": ("own", (1,), "all", "zed", ()),
+    "own0r": ("own", (0,), "all", "right", ()),
+    "own0l": ("own", (0,), "all", "left", ()),
+    "owns": ("own", BOTH, "all", "sib", ()),
+    "z0r": ("z", (0,), "all", "right", ("own0z",)),
+    "z0l": ("z", (0,), "all", "left", ("own0z",)),
+    "z0o": ("z", (0,), "all", "over", ("own0z",)),
+    "l1z": ("l", (1,), "all", "zed", ("own1r",)),
+    "r1z": ("r", (1,), "all", "zed", ("own1l",)),
+    "o1z": ("o", (1,), "all", "zed", ("own1o",)),
+    "l0r": ("l", (0,), "lo", "right", ("own0r",)),
+    "r0l": ("r", (0,), "hi", "left", ("own0l",)),
+    "zs": ("z", BOTH, "all", "sib", ("own0z", "own1z")),
+    "ls": ("l", BOTH, "all", "sib", ("own1r", "own0r")),
+    "rs": ("r", BOTH, "all", "sib", ("own1l", "own0l")),
+    "lzs": ("lz", BOTH, "all", "sib", ("z0r", "l1z")),
+    "rzs": ("rz", BOTH, "all", "sib", ("z0l", "r1z")),
+    "os": ("o", BOTH, "all", "sib", ("own1o", "l0r", "r0l")),
+    "ozs": ("oz", BOTH, "all", "sib", ("z0o", "o1z")),
 }
 EVENTS = len(GATHER)
+ORDER = ("own0z", "own1r", "own1l", "own1z", "own1o", "own0r", "own0l", "z0r", "l1z", "z0l", "r1z", "l0r", "r0l", "z0o", "o1z")
 
 FAR = sorted(
     ((dz, dy) for dz in range(4) for dy in range(8) if dz or dy),
@@ -60,7 +66,7 @@
     tm = lax.axis_index("tm")
 
     z_hi, y = feed // 8, lax.rem(feed, 8)
-    after, before = lax.rem(tm + 1, NT), lax.rem(tm + NT - 1, NT)
+    after = lax.rem(tm + 1, NT)
 
     def feed_at(dz, dy):
         return lax.rem(z_hi + dz, 4) * 8 + lax.rem(y + dy, 8)
@@ -84,7 +90,6 @@
         load.start()
         loads.append(load)
     for step in FAR:
-        greet(feed_at(*step), before)
         greet(feed_at(*step), tm)
     for step in range(1, NT):
         greet(feed, lax.rem(tm + step, NT))
@@ -131,9 +136,11 @@
     sub8 = lax.broadcasted_iota(jnp.int32, (8, 128), 0)
     count_buf[tm] = jnp.where(sub8 < 4, counts[0], counts[1])
 
-    for load in loads:
+    for load in loads[:4]:
         load.wait()
-    prod[...] = lax.dot_general(frames[...], table[...], nt, preferred_element_type=f32)
+    prod[pl.ds(256, 256), :] = lax.dot_general(
+        frames[pl.ds(256, 256), :], table[...], nt, preferred_element_type=f32
+    )
 
     def term(f, t):
         return prod[pl.ds(f * INPUTS, INPUTS), pl.ds(t * NCHAN, NCHAN)]
@@ -145,35 +152,45 @@
             total = total + other
         return total
 
-    for j in range(2):
-        last = partial(FRAMES + 2 * j + 1) if j == 0 else jnp.zeros((INPUTS, NCHAN), f32)
-        turned = jnp.concatenate([partial(FRAMES + 2 * j), last], axis=0).T
-        for q in range(4):
-            next_buf[:, (q // 2) * 4 + (q % 2) * 2 + j, :] = turned[q * NF : (q + 1) * NF, :]
-    for j in range(4):
-        turned = jnp.concatenate([partial(2 * j), partial(2 * j + 1)], axis=0).T
+    for s in range(3):
+        next_buf[pl.ds(s * INPUTS, INPUTS), :] = partial(FRAMES + s).astype(next_buf.dtype)
+    pl.semaphore_wait(barrier, NF - 1 + NT - 1)
+    halo = pltpu.make_async_remote_copy(
+        src_ref=next_buf, dst_ref=prev_buf, send_sem=next_sem.at[0], recv_sem=next_sem.at[1],
+        device_id={"tm": after}, device_id_type=MESH,
+    )
+    halo.start()
+    for load in loads[4:]:
+        load.wait()
+    prod[pl.ds(0, 256), :] = lax.dot_general(
+        frames[pl.ds(0, 256), :], table[...], nt, preferred_element_type=f32
+    )
+
+    def total(s):
+        value = partial(s)
+        if s < 3:
+            value = value + jnp.where(tm > 0, prev_buf[pl.ds(s * INPUTS, INPUTS), :].astype(f32), 0.0)
+        return value
+
+    def turn(j):
+        turned = jnp.concatenate([total(2 * j), total(2 * j + 1)], axis=0).T
         for q in range(4):
             rows[:, (q // 2) * 8 + (j // 2) * 4 + (q % 2) * 2 + j % 2, :] = turned[q * NF : (q + 1) * NF, :]
+
+    turn(3)
+    turn(2)
+    halo.wait_recv()
+    turn(1)
+    turn(0)
     send_buf[...] = rows[...].astype(bf16)
-
-    pl.semaphore_wait(barrier, 2 * (NF - 1) + NT - 1)
-
-    def send_next(peer):
-        pltpu.make_async_remote_copy(
-            src_ref=next_buf.at[peer], dst_ref=prev_buf.at[feed],
-            send_sem=next_sem.at[0], recv_sem=next_sem.at[1],
-            device_id={"feed": peer, "tm": after}, device_id_type=MESH,
-        ).start()
 
     for step in FAR:
         peer = feed_at(*step)
-        send_next(peer)
         pltpu.make_async_remote_copy(
             src_ref=send_buf.at[peer], dst_ref=recv_buf.at[feed],
             send_sem=turn_sem.at[0], recv_sem=turn_sem.at[1],
             device_id={"feed": peer, "tm": tm}, device_id_type=MESH,
         ).start()
-    send_next(feed)
     own = pltpu.make_async_copy(send_buf.at[feed], recv_buf.at[feed], own_sem.at[0])
     own.start()
 
@@ -198,19 +215,11 @@
     own.wait()
     others = recv_buf.at[pl.ds(0, NF - 1)]
     pltpu.make_async_copy(others, others, turn_sem.at[1]).wait()
-    pltpu.make_async_copy(prev_buf, prev_buf, next_sem.at[1]).wait()
 
     low = lax.broadcasted_iota(jnp.int32, (16, 128), 1) < INPUTS
-    top = jnp.logical_and(lax.broadcasted_iota(jnp.int32, (8, 128), 0) < 4, tm > 0)
-
-    def received(f):
-        prev = prev_buf[f]
-        both = jnp.concatenate([jnp.where(top, prev, 0.0), jnp.where(top, pltpu.roll(prev, 4, 0), 0.0)], axis=0)
-        return recv_buf[f].astype(f32) + both
-
     for g in range(NF // 2):
-        one = received(2 * g)
-        two = received(2 * g + 1)
+        one = recv_buf[2 * g].astype(f32)
+        two = recv_buf[2 * g + 1].astype(f32)
         first = jnp.where(low, one, pltpu.roll(two, INPUTS, 1)) * clean[:16]
         second = jnp.where(low, pltpu.roll(one, INPUTS, 1), two) * clean[16:]
         for kl in range(2):
@@ -222,69 +231,59 @@
     def at(dx, dz, dc):
         return lax.rem(x + dx, 4) * 4 + lax.rem(zed + dz, 2) * 2 + lax.rem(core + dc, 2)
 
-    targets = {"sib": at(0, 0, 1), "zed": at(0, 1, 0), "right": at(1, 0, 0), "left": at(3, 0, 0)}
+    targets = {"sib": at(0, 0, 1), "zed": at(0, 1, 0), "right": at(1, 0, 0), "left": at(3, 0, 0), "over": at(2, 0, 0),
+               "rightz": at(1, 1, 0), "leftz": at(3, 1, 0), "overz": at(2, 1, 0)}
     blocks = {"own": (0, 0), "z": (0, 1), "l": (3, 0), "r": (1, 0), "lz": (3, 1), "rz": (1, 1), "o": (2, 0), "oz": (2, 1)}
-    moves = {"sib": (0, 0, 1), "zed": (0, 1, 0), "right": (3, 0, 0), "left": (1, 0, 0)}
+    moves = {"sib": (0, 0, 1), "zed": (0, 1, 0), "right": (3, 0, 0), "left": (1, 0, 0), "over": (2, 0, 0),
+             "rightz": (3, 1, 0), "leftz": (1, 1, 0), "overz": (2, 1, 0)}
     lanes = {"all": pl.ds(0, COLS), "lo": pl.ds(0, HALF), "hi": pl.ds(HALF, HALF)}
-
-    def view(kl, index, which):
-        return full.at[kl, index, :, lanes[which]]
-
-    def send(kl, event):
-        block, which, target = GATHER[event]
-        ref = view(kl, at(*blocks[block], 0), which)
-        copy = pltpu.make_async_remote_copy(
+    numbers = {name: n for n, name in enumerate(GATHER)}
+
+    def view(index, chans, which):
+        return full.at[pl.ds(chans[0], len(chans)), index, :, lanes[which]]
+
+    def send(name):
+        block, chans, which, target, _ = GATHER[name]
+        ref = view(at(*blocks[block], 0), chans, which)
+        pltpu.make_async_remote_copy(
             src_ref=ref, dst_ref=ref,
-            send_sem=gather_send.at[kl, event], recv_sem=gather_recv.at[kl, event],
+            send_sem=gather_send.at[numbers[name]], recv_sem=gather_recv.at[numbers[name]],
             device_id={"tm": targets[target]}, device_id_type=MESH,
-        )
-        copy.start()
-
-    def arrived(kl, event):
-        block, which, target = GATHER[event]
+        ).start()
+
+    def arrived(name):
+        block, chans, which, target, _ = GATHER[name]
         dx, dz = blocks[block]
         mx, mz, mc = moves[target]
-        ref = view(kl, at((dx + mx) % 4, (dz + mz) % 2, mc), which)
-        pltpu.make_async_copy(ref, ref, gather_recv.at[kl, event]).wait()
-
-    def sent(kl, event):
-        block, which, _ = GATHER[event]
-        ref = view(kl, at(*blocks[block], 0), which)
-        pltpu.make_async_copy(ref, ref, gather_send.at[kl, event]).wait()
-
-    def relay(kl, event, *following):
-        arrived(kl, event)
-        for after in following:
-            send(kl, after)
-
-    for kl in range(2):
-        for event in (2, 3, 1, 0):
-            send(kl, event)
-    for kl in range(2):
-        relay(kl, 1, 5, 6, 4)
-        relay(kl, 2, 8, 7)
-        relay(kl, 3, 10, 9)
-    for kl in range(2):
-        relay(kl, 5, 12, 11)
-        relay(kl, 6, 14, 13)
-
-    for kl in range(2):
-        relay(kl, 8, 15)
-        relay(kl, 10, 16)
-        relay(kl, 12, 17)
-        relay(kl, 14, 18)
+        ref = view(at((dx + mx) % 4, (dz + mz) % 2, mc), chans, which)
+        pltpu.make_async_copy(ref, ref, gather_recv.at[numbers[name]]).wait()
+
+    def sent(name):
+        block, chans, which, _, _ = GATHER[name]
+        ref = view(at(*blocks[block], 0), chans, which)
+        pltpu.make_async_copy(ref, ref, gather_send.at[numbers[name]]).wait()
+
+    here = set()
+    for name in GATHER:
+        if not GATHER[name][4]:
+            send(name)
+    for name in ORDER:
+        arrived(name)
+        here.add(name)
+        for later in GATHER:
+            if name in GATHER[later][4] and here.issuperset(GATHER[later][4]):
+                send(later)
     every = count_buf.at[pl.ds(0, NT - 1)]
     pltpu.make_async_copy(every, every, count_sem.at[1]).wait()
-    for kl in range(2):
-        for event in (0, 4, 7, 9, 11, 13, 15, 16, 17, 18):
-            arrived(kl, event)
+    for name in GATHER:
+        if name not in ORDER:
+            arrived(name)
     pltpu.make_async_copy(every, every, count_sem.at[0]).wait()
     gone = send_buf.at[pl.ds(0, NF - 1)]
     pltpu.make_async_copy(gone, gone, turn_sem.at[0]).wait()
-    pltpu.make_async_copy(next_buf, next_buf, next_sem.at[0]).wait()
-    for kl in range(2):
-        for event in range(EVENTS):
-            sent(kl, event)
+    halo.wait_send()
+    for name in GATHER:
+        sent(name)
 
 
 def correlate(full, count_buf, out_re, out_im, stage_re, stage_im, store_sem):
@@ -336,15 +335,15 @@
             pltpu.VMEM((NF, 16, 128), f32),
             pltpu.VMEM((NF, 16, 128), bf16),
             pltpu.VMEM((NF, 16, 128), bf16),
-            pltpu.VMEM((NF, 8, 128), f32),
-            pltpu.VMEM((NF, 8, 128), f32),
+            pltpu.VMEM((3 * INPUTS, NCHAN), f32),
+            pltpu.VMEM((3 * INPUTS, NCHAN), f32),
             dma((3,)),
             dma((FRAMES,)),
             dma((2,)),
             dma((2,)),
             dma((2,)),
-            dma((2, EVENTS)),
-            dma((2, EVENTS)),
+            dma((EVENTS,)),
+            dma((EVENTS,)),
             dma((1,)),
         ],
         compiler_params=pltpu.CompilerParams(

time: 43.3 us -> 40.5 us (0.935)
  Pallas kernels: 42.5 us -> 39.7 us
    pallas_call x1, Pallas kernels: 40.8 us -> 38 us  [body(): pl.pallas_call(kernel, out_shape=(jax.ShapeDtypeStruct((2, NT, 16, COLS),...]
where the time goes in v3:
time: 40.5 us; the launch traced here: 40.3 us
  Pallas kernels  39.7 us (98%)
  between operations  0.64 us (2%)
    pallas_call x1, Pallas kernels, body(): pl.pallas_call(kernel, out_shape=(jax.ShapeDtypeStruct((2, NT, 16, COLS),...  38 us
    pallas_call x1, Pallas kernels, body(): pl.pallas_call(correlate, out_shape=(out, out), in_specs=[vmem, vmem], ou...  1.7 us

profile of v3, /device:TPU:1, one launch (start us, length us, event | category | flops | bytes accessed | tf_op | source)
XLA Modules:
  0.0 40.3 jit_solution(10400901734472833816)
XLA Ops:
  0.6 38.0 %channelize_gather.1 = (bf16[2,16,16,2048]{3,2,1,0:T(8,128)(2,1)S(1)}, f32[16,8,128]{2,1,0:T(8,128)S(1)}) custom-call(bf16[64,16384]{1,0:T(8,128)(2,1)} %volt.1, f32[4,2048]{1,0:T(4,128)} %coef_hbm.1, s32[8,64]{1,0:T(8,128)} %flags_hbm.1, s32[1,64]{1,0:T(1,128)} %bitcast.1), custom_call_target="tpu_custom_call" | custom-call | tf_op jit(solution)/shard_map/channelize_gather/pallas_call | solution.py:323
  38.6 1.7 %correlate.1 = (bf16[2,128,2048]{2,1,0:T(8,128)(2,1)}, bf16[2,128,2048]{2,1,0:T(8,128)(2,1)}) custom-call(bf16[2,16,16,2048]{3,2,1,0:T(8,128)(2,1)S(1)} %get-tuple-element.4.full, f32[16,8,128]{2,1,0:T(8,128)S(1)} %get-tuple-element.5.count_buf), custom_call_target="tpu_custom_call" | custom-call | tf_op jit(solution)/shard_map/correlate/pallas_call | solution.py:355

commit v4 on v3

--- a/solution.py
+++ b/solution.py
@@ -49,6 +49,7 @@
     "ozs": ("oz", BOTH, "all", "sib", ("z0o", "o1z")),
 }
 EVENTS = len(GATHER)
+PLACE = {"own": 0, "r": 1, "o": 2, "l": 3, "z": 4, "rz": 5, "oz": 6, "lz": 7}
 ORDER = ("own0z", "own1r", "own1l", "own1z", "own1o", "own0r", "own0l", "z0r", "l1z", "z0l", "r1z", "l0r", "r0l", "z0o", "o1z")
 
 FAR = sorted(
@@ -76,6 +77,8 @@
     def greet(feed_to, tm_to):
         pl.semaphore_signal(barrier, inc=1, device_id={"feed": feed_to, "tm": tm_to}, device_id_type=MESH)
 
+    for step in FAR[:8]:
+        greet(feed_at(*step), tm)
     smalls = [
         pltpu.make_async_copy(src, dst, small_sem.at[n])
         for n, (src, dst) in enumerate(((order_hbm, order), (coef_hbm, coef), (flags_hbm, flags)))
@@ -89,7 +92,7 @@
         )
         load.start()
         loads.append(load)
-    for step in FAR:
+    for step in FAR[8:]:
         greet(feed_at(*step), tm)
     for step in range(1, NT):
         greet(feed, lax.rem(tm + step, NT))
@@ -106,24 +109,31 @@
     freq = jnp.broadcast_to(chan_of + CHAN0, (NCHAN, 128))
     lane = lax.broadcasted_iota(jnp.int32, (NCHAN, 128), 1)
     part = (lax.broadcasted_iota(jnp.int32, (NCHAN, 128), 0) >> 5) & 1
-    phase0 = freq * lane + part * (FRAME // 4)
-    phase_step = freq * 128
     scale = (TAPS * FRAME / 2.0) ** (-0.5)
 
-    def table_block(a, phase):
-        cols = pl.ds(pl.multiple_of(a * 128, 128), 128)
+    def trig(phase):
         dist = jnp.abs((phase & (FRAME - 1)) - FRAME // 2).astype(f32)
         z = dist * (4.0 / FRAME) - 1.0
         z2 = z * z
-        trig = jnp.full_like(z, SINE[-1])
-        for term in SINE[-2::-1]:
-            trig = trig * z2 + term
-        trig = trig * z
+        value = jnp.full_like(z, SINE[-1])
+        for power in SINE[-2::-1]:
+            value = value * z2 + power
+        return value * z
+
+    quarter = FRAME // 4
+    first = trig(freq * lane + part * quarter)
+    turn_cos = trig(freq * 128)
+    turn_sin = trig(freq * 128 - quarter)
+    signed = jnp.where(part == 0, turn_sin, -turn_sin)
+
+    def table_block(a, value):
+        cols = pl.ds(pl.multiple_of(a * 128, 128), 128)
         for t in range(TAPS):
-            table[pl.ds(t * NCHAN, NCHAN), cols] = (trig * (coef[pl.ds(t, 1), cols] * scale)).astype(bf16)
-        return phase + phase_step
-
-    lax.fori_loop(0, FRAME // 128, table_block, phase0)
+            table[pl.ds(t * NCHAN, NCHAN), cols] = (value * (coef[pl.ds(t, 1), cols] * scale)).astype(bf16)
+        swapped = jnp.concatenate([value[n * NF : (n + 1) * NF] for n in (1, 0, 3, 2)], axis=0)
+        return value * turn_cos + swapped * signed
+
+    lax.fori_loop(0, FRAME // 128, table_block, first)
 
     hot = (lax.broadcasted_iota(jnp.int32, (NCHAN, 2 * NF), 1) == chan_of).astype(bf16)
     nt = (((1,), (1,)), ((), ()))
@@ -159,7 +169,10 @@
         src_ref=next_buf, dst_ref=prev_buf, send_sem=next_sem.at[0], recv_sem=next_sem.at[1],
         device_id={"tm": after}, device_id_type=MESH,
     )
-    halo.start()
+    @pl.when(tm < NT - 1)
+    def _():
+        halo.start()
+
     for load in loads[4:]:
         load.wait()
     prod[pl.ds(0, 256), :] = lax.dot_general(
@@ -179,7 +192,10 @@
 
     turn(3)
     turn(2)
-    halo.wait_recv()
+    @pl.when(tm > 0)
+    def _():
+        halo.wait_recv()
+
     turn(1)
     turn(0)
     send_buf[...] = rows[...].astype(bf16)
@@ -224,44 +240,42 @@
         second = jnp.where(low, pltpu.roll(one, INPUTS, 1), two) * clean[16:]
         for kl in range(2):
             block = jnp.concatenate([first[kl * 8 : kl * 8 + 8], second[kl * 8 : kl * 8 + 8]], axis=0)
-            full[kl, tm, :, pl.ds(g * 128, 128)] = block.astype(bf16)
+            full[kl, 0, :, pl.ds(g * 128, 128)] = block.astype(bf16)
 
     x, zed, core = tm // 4, lax.rem(tm // 2, 2), lax.rem(tm, 2)
-
-    def at(dx, dz, dc):
-        return lax.rem(x + dx, 4) * 4 + lax.rem(zed + dz, 2) * 2 + lax.rem(core + dc, 2)
-
-    targets = {"sib": at(0, 0, 1), "zed": at(0, 1, 0), "right": at(1, 0, 0), "left": at(3, 0, 0), "over": at(2, 0, 0),
-               "rightz": at(1, 1, 0), "leftz": at(3, 1, 0), "overz": at(2, 1, 0)}
-    blocks = {"own": (0, 0), "z": (0, 1), "l": (3, 0), "r": (1, 0), "lz": (3, 1), "rz": (1, 1), "o": (2, 0), "oz": (2, 1)}
-    moves = {"sib": (0, 0, 1), "zed": (0, 1, 0), "right": (3, 0, 0), "left": (1, 0, 0), "over": (2, 0, 0),
-             "rightz": (3, 1, 0), "leftz": (1, 1, 0), "overz": (2, 1, 0)}
+    targets = {
+        "sib": (x, zed, 1 - core),
+        "zed": (x, 1 - zed, core),
+        "right": (lax.rem(x + 1, 4), zed, core),
+        "left": (lax.rem(x + 3, 4), zed, core),
+        "over": (lax.rem(x + 2, 4), zed, core),
+    }
+    targets = {name: tx * 4 + tz * 2 + tc for name, (tx, tz, tc) in targets.items()}
+    moves = {"sib": (0, 0, 8), "zed": (0, 4, 0), "right": (3, 0, 0), "left": (1, 0, 0), "over": (2, 0, 0)}
     lanes = {"all": pl.ds(0, COLS), "lo": pl.ds(0, HALF), "hi": pl.ds(HALF, HALF)}
-    numbers = {name: n for n, name in enumerate(GATHER)}
-
-    def view(index, chans, which):
-        return full.at[pl.ds(chans[0], len(chans)), index, :, lanes[which]]
+    across = [name for name in GATHER if GATHER[name][3] != "sib"]
+    numbers = {name: across.index(name) if name in across else len(across) for name in GATHER}
+
+    def sent_view(name):
+        block, chans, which, _, _ = GATHER[name]
+        return full.at[pl.ds(chans[0], len(chans)), PLACE[block], :, lanes[which]]
+
+    def arrived_view(name):
+        block, chans, which, target, _ = GATHER[name]
+        place, (dx, dz, dc) = PLACE[block], moves[target]
+        place = (place % 4 + dx) % 4 + (place // 4 * 4 + dz) % 8 + dc
+        return full.at[pl.ds(chans[0], len(chans)), place, :, lanes[which]]
 
     def send(name):
-        block, chans, which, target, _ = GATHER[name]
-        ref = view(at(*blocks[block], 0), chans, which)
         pltpu.make_async_remote_copy(
-            src_ref=ref, dst_ref=ref,
-            send_sem=gather_send.at[numbers[name]], recv_sem=gather_recv.at[numbers[name]],
-            device_id={"tm": targets[target]}, device_id_type=MESH,
+            src_ref=sent_view(name), dst_ref=arrived_view(name),
+            send_sem=gather_send, recv_sem=gather_recv.at[numbers[name]],
+            device_id={"tm": targets[GATHER[name][3]]}, device_id_type=MESH,
         ).start()
 
     def arrived(name):
-        block, chans, which, target, _ = GATHER[name]
-        dx, dz = blocks[block]
-        mx, mz, mc = moves[target]
-        ref = view(at((dx + mx) % 4, (dz + mz) % 2, mc), chans, which)
+        ref = arrived_view(name)
         pltpu.make_async_copy(ref, ref, gather_recv.at[numbers[name]]).wait()
-
-    def sent(name):
-        block, chans, which, _, _ = GATHER[name]
-        ref = view(at(*blocks[block], 0), chans, which)
-        pltpu.make_async_copy(ref, ref, gather_send.at[numbers[name]]).wait()
 
     here = set()
     for name in GATHER:
@@ -275,15 +289,21 @@
                 send(later)
     every = count_buf.at[pl.ds(0, NT - 1)]
     pltpu.make_async_copy(every, every, count_sem.at[1]).wait()
-    for name in GATHER:
+    for name in across:
         if name not in ORDER:
             arrived(name)
+    sibling = full.at[:, pl.ds(NT // 2, NT // 2)]
+    pltpu.make_async_copy(sibling, sibling, gather_recv.at[len(across)]).wait()
     pltpu.make_async_copy(every, every, count_sem.at[0]).wait()
     gone = send_buf.at[pl.ds(0, NF - 1)]
     pltpu.make_async_copy(gone, gone, turn_sem.at[0]).wait()
-    halo.wait_send()
-    for name in GATHER:
-        sent(name)
+    @pl.when(tm < NT - 1)
+    def _():
+        halo.wait_send()
+
+    units = sum(len(chans) * (2 if which == "all" else 1) for _, chans, which, _, _ in GATHER.values())
+    all_sent = full.at[:, pl.ds(0, units // 4)]
+    pltpu.make_async_copy(all_sent, all_sent, gather_send).wait()
 
 
 def correlate(full, count_buf, out_re, out_im, stage_re, stage_im, store_sem):
@@ -342,7 +362,7 @@
             dma((2,)),
             dma((2,)),
             dma((2,)),
-            dma((EVENTS,)),
+            dma,
             dma((EVENTS,)),
             dma((1,)),
         ],

time: 40.5 us -> 39.7 us (0.980)
  Pallas kernels: 39.7 us -> 38.9 us
    pallas_call x1, Pallas kernels: 38 us -> 37.2 us  [body(): pl.pallas_call(kernel, out_shape=(jax.ShapeDtypeStruct((2, NT, 16, COLS),...]
where the time goes in v4:
time: 39.7 us; the launch traced here: 39.6 us
  Pallas kernels  38.9 us (98%)
  between operations  0.64 us (2%)
    pallas_call x1, Pallas kernels, body(): pl.pallas_call(kernel, out_shape=(jax.ShapeDtypeStruct((2, NT, 16, COLS),...  37.2 us
    pallas_call x1, Pallas kernels, body(): pl.pallas_call(correlate, out_shape=(out, out), in_specs=[vmem, vmem], ou...  1.7 us

profile of v4, /device:TPU:1, one launch (start us, length us, event | category | flops | bytes accessed | tf_op | source)
XLA Modules:
  0.0 39.6 jit_solution(6440894303539473008)
XLA Ops:
  0.6 37.2 %channelize_gather.1 = (bf16[2,16,16,2048]{3,2,1,0:T(8,128)(2,1)S(1)}, f32[16,8,128]{2,1,0:T(8,128)S(1)}) custom-call(bf16[64,16384]{1,0:T(8,128)(2,1)} %volt.1, f32[4,2048]{1,0:T(4,128)} %coef_hbm.1, s32[8,64]{1,0:T(8,128)} %flags_hbm.1, s32[1,64]{1,0:T(1,128)} %bitcast.1), custom_call_target="tpu_custom_call" | custom-call | tf_op jit(solution)/shard_map/channelize_gather/pallas_call | solution.py:343
  37.9 1.7 %correlate.1 = (bf16[2,128,2048]{2,1,0:T(8,128)(2,1)}, bf16[2,128,2048]{2,1,0:T(8,128)(2,1)}) custom-call(bf16[2,16,16,2048]{3,2,1,0:T(8,128)(2,1)S(1)} %get-tuple-element.4.full, f32[16,8,128]{2,1,0:T(8,128)S(1)} %get-tuple-element.5.count_buf), custom_call_target="tpu_custom_call" | custom-call | tf_op jit(solution)/shard_map/correlate/pallas_call | solution.py:375

commit v5 on v4

--- a/solution.py
+++ b/solution.py
@@ -355,8 +355,8 @@
             pltpu.VMEM((NF, 16, 128), f32),
             pltpu.VMEM((NF, 16, 128), bf16),
             pltpu.VMEM((NF, 16, 128), bf16),
-            pltpu.VMEM((3 * INPUTS, NCHAN), f32),
-            pltpu.VMEM((3 * INPUTS, NCHAN), f32),
+            pltpu.VMEM((3 * INPUTS, NCHAN), bf16),
+            pltpu.VMEM((3 * INPUTS, NCHAN), bf16),
             dma((3,)),
             dma((FRAMES,)),
             dma((2,)),

time: 39.7 us -> 39.2 us (0.987)
  Pallas kernels: 38.9 us -> 38.4 us
    pallas_call x1, Pallas kernels: 37.2 us -> 36.7 us  [body(): pl.pallas_call(kernel, out_shape=(jax.ShapeDtypeStruct((2, NT, 16, COLS),...]
where the time goes in v5:
time: 39.2 us; the launch traced here: 39 us
  Pallas kernels  38.4 us (98%)
  between operations  0.64 us (2%)
    pallas_call x1, Pallas kernels, body(): pl.pallas_call(kernel, out_shape=(jax.ShapeDtypeStruct((2, NT, 16, COLS),...  36.7 us
    pallas_call x1, Pallas kernels, body(): pl.pallas_call(correlate, out_shape=(out, out), in_specs=[vmem, vmem], ou...  1.7 us

profile of v5, /device:TPU:1, one launch (start us, length us, event | category | flops | bytes accessed | tf_op | source)
XLA Modules:
  0.0 39.0 jit_solution(6459699309717622238)
XLA Ops:
  0.6 36.7 %channelize_gather.1 = (bf16[2,16,16,2048]{3,2,1,0:T(8,128)(2,1)S(1)}, f32[16,8,128]{2,1,0:T(8,128)S(1)}) custom-call(bf16[64,16384]{1,0:T(8,128)(2,1)} %volt.1, f32[4,2048]{1,0:T(4,128)} %coef_hbm.1, s32[8,64]{1,0:T(8,128)} %flags_hbm.1, s32[1,64]{1,0:T(1,128)} %bitcast.1), custom_call_target="tpu_custom_call" | custom-call | tf_op jit(solution)/shard_map/channelize_gather/pallas_call | solution.py:343
  37.3 1.7 %correlate.1 = (bf16[2,128,2048]{2,1,0:T(8,128)(2,1)}, bf16[2,128,2048]{2,1,0:T(8,128)(2,1)}) custom-call(bf16[2,16,16,2048]{3,2,1,0:T(8,128)(2,1)S(1)} %get-tuple-element.4.full, f32[16,8,128]{2,1,0:T(8,128)S(1)} %get-tuple-element.5.count_buf), custom_call_target="tpu_custom_call" | custom-call | tf_op jit(solution)/shard_map/correlate/pallas_call | solution.py:375

commit v6 on v5

--- a/solution.py
+++ b/solution.py
@@ -146,10 +146,10 @@
     sub8 = lax.broadcasted_iota(jnp.int32, (8, 128), 0)
     count_buf[tm] = jnp.where(sub8 < 4, counts[0], counts[1])
 
-    for load in loads[:4]:
+    for load in loads[:3]:
         load.wait()
-    prod[pl.ds(256, 256), :] = lax.dot_general(
-        frames[pl.ds(256, 256), :], table[...], nt, preferred_element_type=f32
+    prod[pl.ds(320, 192), pl.ds(0, 384)] = lax.dot_general(
+        frames[pl.ds(320, 192), :], table[pl.ds(0, 384), :], nt, preferred_element_type=f32
     )
 
     def term(f, t):
@@ -173,10 +173,13 @@
     def _():
         halo.start()
 
-    for load in loads[4:]:
+    for load in loads[3:]:
         load.wait()
-    prod[pl.ds(0, 256), :] = lax.dot_general(
-        frames[pl.ds(0, 256), :], table[...], nt, preferred_element_type=f32
+    prod[pl.ds(0, 320), :] = lax.dot_general(
+        frames[pl.ds(0, 320), :], table[...], nt, preferred_element_type=f32
+    )
+    prod[pl.ds(320, 192), pl.ds(384, 128)] = lax.dot_general(
+        frames[pl.ds(320, 192), :], table[pl.ds(384, 128), :], nt, preferred_element_type=f32
     )
 
     def total(s):

time: 39.2 us -> 39.2 us (level)
  no operation moved by 1% of the time
where the time goes in v6:
time: 39.2 us; the launch traced here: 39.1 us
  Pallas kernels  38.4 us (98%)
  between operations  0.64 us (2%)
    pallas_call x1, Pallas kernels, body(): pl.pallas_call(kernel, out_shape=(jax.ShapeDtypeStruct((2, NT, 16, COLS),...  36.7 us
    pallas_call x1, Pallas kernels, body(): pl.pallas_call(correlate, out_shape=(out, out), in_specs=[vmem, vmem], ou...  1.7 us

profile of v6, /device:TPU:1, one launch (start us, length us, event | category | flops | bytes accessed | tf_op | source)
XLA Modules:
  0.0 39.1 jit_solution(7450746032669964409)
XLA Ops:
  0.6 36.7 %channelize_gather.1 = (bf16[2,16,16,2048]{3,2,1,0:T(8,128)(2,1)S(1)}, f32[16,8,128]{2,1,0:T(8,128)S(1)}) custom-call(bf16[64,16384]{1,0:T(8,128)(2,1)} %volt.1, f32[4,2048]{1,0:T(4,128)} %coef_hbm.1, s32[8,64]{1,0:T(8,128)} %flags_hbm.1, s32[1,64]{1,0:T(1,128)} %bitcast.1), custom_call_target="tpu_custom_call" | custom-call | tf_op jit(solution)/shard_map/channelize_gather/pallas_call | solution.py:346
  37.4 1.7 %correlate.1 = (bf16[2,128,2048]{2,1,0:T(8,128)(2,1)}, bf16[2,128,2048]{2,1,0:T(8,128)(2,1)}) custom-call(bf16[2,16,16,2048]{3,2,1,0:T(8,128)(2,1)S(1)} %get-tuple-element.4.full, f32[16,8,128]{2,1,0:T(8,128)S(1)} %get-tuple-element.5.count_buf), custom_call_target="tpu_custom_call" | custom-call | tf_op jit(solution)/shard_map/correlate/pallas_call | solution.py:378
